TPU v7x, 32 devices: a whole 2x2x4 slice. The times are simulated.
32 devices in a mesh: ax: 4 (over z), az: 8 (over y, x, core).
Axes of the slice: x: 2, y: 2, z: 4, core: 2. Of those that a mesh axis runs over, the one named last changes fastest.
Arguments:
- adjoint: float32 [3, 128, 512, 256], P(None, 'ax', 'az'), may hold values from -6 to 6
- primal: float32 [3, 128, 512, 256], P(None, 'ax', 'az'), may hold values from -6 to 6
- wall: int32 [128, 512], P('ax', 'az'), may hold values from 0 to 63
- owner: int32 [128, 512], P('ax', 'az'), may hold values from 0 to 1023, as said below
- adjacency: int32 [4, 256, 4], P('ax', 'az'), may hold values from 0 to 95
- counts: int32 [4, 256], P('ax', 'az'), may hold values from 32 to 128
- laplacian: float32 [4, 256, 128, 128], P('ax', 'az'), as said below
Outputs:
- adjoint_next: float32 [3, 128, 512, 256], P(None, 'ax', 'az')
- smoothed: float32 [4, 256, 128], P('ax', 'az')
Inputs may be any that keep to these rules, and one draw needn't show every extreme that they name: `owner`: patch p lives on device p // 32 of the mesh in order ax then az. Among the columns of one device, at most 192 have owners on one device, and in every draw some owning devices receive exactly 192 from every device. `laplacian`: diagonal entries lie in 2 to 3, off-diagonal ones in -2 / 128 to 0.
All inputs are finite; a program needn't handle non-finite values.
Results may differ from a plain program's by a relative error of at most 0.0001.
Values sent between devices are 32-bit elements; how exact they have to be, the bound alone decides.
A program may use at most 128 MiB of HBM per device.

v0:
```python
import functools

import jax
import jax.numpy as jnp
from jax import lax
from jax.experimental import pallas as pl
from jax.experimental.pallas import tpu as pltpu
from jax.sharding import PartitionSpec as P

SWEEPS = 3

time_step = 0.12
viscosity = 1.0
wall_scale = 0.1
smoothing = 0.5
coupling = 0.25
relaxation = 0.25

F32 = jnp.float32
BF16 = jnp.bfloat16
MESH = pl.DeviceIdType.MESH
PAD = 8


def pieces(value):
    high = value.astype(BF16).astype(F32)
    return high, value - high


def column_of(row):
    n = row.shape[1]
    eye = lax.broadcasted_iota(jnp.int32, (n, n), 0) == lax.broadcasted_iota(jnp.int32, (n, n), 1)
    return jnp.sum(jnp.where(eye, jnp.broadcast_to(row, (n, n)), 0.0), axis=1, keepdims=True)


def stencil_kernel(
    planes, adjoint, primal, wall, x_low, x_high, a_low, a_high, out, tiles, held, depth_of, sems
):
    step = pl.program_id(0)
    axial, sector, radial = adjoint.shape[1:]
    vertices = tiles.shape[-1] // 2
    rows = 8

    def fetch(x):
        return pltpu.make_async_copy(
            adjoint.at[:, x], held.at[:, x + 1, pl.ds(PAD, sector), :], sems.at[x]
        )

    def side_rows(x):
        for c in range(3):
            held[c, x + 1, PAD - 1 : PAD, :] = a_low[c, pl.ds(x, 1), :]
            held[c, x + 1, PAD + sector : PAD + sector + 1, :] = a_high[c, pl.ds(x, 1), :]

    @pl.when(step == 0)
    def _():
        def begin(x, carry):
            fetch(x).start()
            return carry

        lax.fori_loop(0, axial, begin, 0)
        for c in range(3):
            held[c, 0, PAD : PAD + sector, :] = x_low[c]
            held[c, axial + 1, PAD : PAD + sector, :] = x_high[c]
        depths = wall[...].astype(F32)
        for x in range(axial):
            column = column_of(depths[x : x + 1, :])
            depth_of[x] = jnp.broadcast_to(column, depth_of.shape[1:])
        depth_of[axial] = jnp.zeros(depth_of.shape[1:], F32)
        fetch(0).wait()
        side_rows(0)
        full_lane = lax.broadcasted_iota(jnp.int32, (sector, radial), 1).astype(F32)
        solid = full_lane < jnp.concatenate([depth_of[0]] * (radial // vertices), axis=1)
        for c in range(3):
            body = held[c, 1, PAD : PAD + sector, :]
            held[c, 1, PAD : PAD + sector, :] = jnp.where(solid, 0.0, body)

    lane = lax.broadcasted_iota(jnp.int32, (rows, radial), 1)
    sub = lax.broadcasted_iota(jnp.int32, (rows, radial), 0)
    first, last = lane == 0, lane == radial - 1
    top, bottom = sub == 0, sub == rows - 1
    lane_value = lane.astype(F32)

    def plane(j, carry):
        x = step * planes + j

        @pl.when(x + 1 < axial)
        def _():
            fetch(x + 1).wait()
            side_rows(x + 1)

        def fluid_at(x, a):
            depth = depth_of[x, a : a + rows, :]
            return lane_value >= jnp.concatenate([depth] * (radial // vertices), axis=1)

        def block(c, at):
            return held[c, x + 1, at : at + rows, :]

        middles = [block(c, PAD) for c in range(3)]
        downs = [pltpu.roll(block(c, PAD - rows), 1, 0) for c in range(3)]
        ups = [pltpu.roll(middles[c], rows - 1, 0) for c in range(3)]
        highs, lows = [], []
        for a in range(0, sector, rows):
            at = PAD + a
            fluid, fluid_next = fluid_at(x, a), fluid_at(x + 1, a)
            flows = [primal[d, j, a : a + rows, :] for d in range(3)]
            half = [(0.5 * time_step) * flow for flow in flows]
            plus = [viscosity * time_step + value for value in half]
            minus = [viscosity * time_step - value for value in half]
            plus[2] = jnp.where(last, 0.0, plus[2])
            minus[2] = jnp.where(first, 0.0, minus[2])
            total = jnp.zeros((rows, vertices), F32)
            for c in range(3):
                middle = middles[c]
                follow = block(c, at + rows)
                down = pltpu.roll(middle, 1, 0)
                up = pltpu.roll(follow, rows - 1, 0)
                value = (1.0 - 6.0 * viscosity * time_step) * middle
                ahead = jnp.where(fluid_next, held[c, x + 2, at : at + rows, :], 0.0)
                held[c, x + 2, at : at + rows, :] = ahead
                value += plus[0] * ahead
                value += minus[0] * held[c, x, at : at + rows, :]
                value += plus[1] * jnp.where(bottom, up, ups[c])
                value += minus[1] * jnp.where(top, downs[c], down)
                value += plus[2] * pltpu.roll(middle, radial - 1, 1)
                value += minus[2] * pltpu.roll(middle, 1, 1)
                value = jnp.where(fluid, value, 0.0)
                out[c, j, a : a + rows, :] = value
                total += flows[c][:, :vertices] * value[:, :vertices]
                middles[c], downs[c], ups[c] = follow, down, up
            high, low = pieces(total)
            highs.append(high)
            lows.append(low)
        both = [jnp.concatenate(part, axis=0) for part in (highs, lows)]
        tiles[j, 0] = jnp.concatenate(both, axis=1).astype(BF16)
        return carry

    lax.fori_loop(0, planes, plane, 0)


def stencil(adjoint, primal, wall, halos, vertices):
    comps, axial, sector, radial = adjoint.shape
    planes = 4
    steps = axial // planes
    vmem = pl.BlockSpec(memory_space=pltpu.VMEM)
    return pl.pallas_call(
        functools.partial(stencil_kernel, planes),
        grid=(steps,),
        out_shape=(
            jax.ShapeDtypeStruct(adjoint.shape, F32),
            jax.ShapeDtypeStruct((axial // 2, 2, sector, 2 * vertices), BF16),
        ),
        in_specs=[
            pl.BlockSpec(memory_space=pl.ANY),
            pl.BlockSpec((comps, planes, sector, radial), lambda i: (0, i, 0, 0)),
            vmem,
            vmem,
            vmem,
            vmem,
            vmem,
        ],
        out_specs=(
            pl.BlockSpec((comps, planes, sector, radial), lambda i: (0, i, 0, 0)),
            pl.BlockSpec(
                (planes, 1, sector, 2 * vertices),
                lambda i: (i % (steps // 2), i // (steps // 2), 0, 0),
            ),
        ),
        scratch_shapes=[
            pltpu.VMEM((comps, axial + 2, sector + 2 * PAD, radial), F32),
            pltpu.VMEM((axial + 1, sector, vertices), F32),
            pltpu.SemaphoreType.DMA((axial,)),
        ],
        compiler_params=pltpu.CompilerParams(vmem_limit_bytes=60 * 2**20),
        cost_estimate=pl.CostEstimate(
            flops=60 * adjoint.size, bytes_accessed=14 * adjoint.size, transcendentals=0
        ),
        name="stencil",
    )(adjoint, primal, wall, *halos)


def smooth_kernel(
    n_ax,
    n_az,
    tiles_in,
    owner,
    adjacency,
    counts,
    laplacian,
    out,
    tiles,
    matrices,
    pair_out,
    pair_own,
    pair_in,
    plane_sum,
    plane_in,
    axial_out,
    axial_in,
    ring_out,
    ring_in,
    tile_sem,
    matrix_sem,
    pair_sems,
    plane_sems,
    axial_sems,
    ring_sems,
):
    ax, az = lax.axis_index("ax"), lax.axis_index("az")
    patches, vertices = out.shape[1:]
    chips = n_az // 2
    chip, core = az // 2, az % 2
    sibling = chip * 2 + (1 - core)
    after, before = (az + 1) % n_az, (az + n_az - 1) % n_az
    half_rows = chips * patches

    tile_load = pltpu.make_async_copy(tiles_in, tiles, tile_sem)
    tile_load.start()
    load = pltpu.make_async_copy(laplacian, matrices, matrix_sem)
    load.start()

    barrier = pltpu.get_barrier_semaphore()
    partners = [(ax, sibling), (ax, after), (ax, before)]
    partners += [(ax, ((chip + d) % chips) * 2 + core) for d in range(1, chips)]
    partners += [((ax + d) % n_ax, az) for d in range(1, n_ax)]
    for partner in partners:
        pl.semaphore_signal(barrier, inc=1, device_id=partner, device_id_type=MESH)

    columns_half = owner.shape[0] // 2
    owners = jnp.concatenate([owner[:columns_half, :], owner[columns_half:, :]], axis=1)
    width = owners.shape[1]
    row = lax.broadcasted_iota(jnp.int32, (2 * half_rows, width), 0)
    row_core = jnp.where(row < half_rows, 1 - core, core)
    row_chip = (row % half_rows) // patches
    row_patch = (row_chip * 2 + row_core) * patches + row % patches

    def partial_sum(target_ax, first):
        ids = row_patch + target_ax * n_az * patches
        hits = [
            jnp.where(ids == owners[b : b + 1, :], 1.0, 0.0).astype(BF16)
            for b in range(columns_half)
        ]
        if first:
            tile_load.wait()
        both = jnp.dot(jnp.concatenate(hits, axis=1), tiles[...], preferred_element_type=F32)
        return both[:, :vertices] + both[:, vertices:]

    def remote(src, dst, sems, target):
        return pltpu.make_async_remote_copy(
            src_ref=src,
            dst_ref=dst,
            send_sem=sems.at[0],
            recv_sem=sems.at[1],
            device_id=target,
            device_id_type=MESH,
        )

    def pair_copy(t):
        return remote(pair_out.at[t], pair_in.at[t], pair_sems.at[t], (ax, sibling))

    def plane_copy(t, d):
        target = (chip + d) % chips
        return remote(
            plane_sum.at[t, target],
            plane_in.at[t, d - 1],
            plane_sems.at[t, d - 1],
            (ax, target * 2 + core),
        )

    def axial_copy(t):
        return remote(
            axial_out.at[t], axial_in.at[t], axial_sems.at[t], ((ax + 1 + t) % n_ax, az)
        )

    def plane_stage(t):
        pair_copy(t).wait()
        joined = pair_own[t] + pair_in[t]
        plane_sum[t] = joined.reshape(chips, patches, vertices)
        for d in range(1, chips):
            plane_copy(t, d).start()

    def axial_stage(t):
        for d in range(1, chips):
            plane_copy(t, d).wait()
        total = plane_sum[t, chip]
        for d in range(1, chips):
            total += plane_in[t, d - 1]
        axial_out[t] = total
        if t < n_ax - 1:
            axial_copy(t).start()

    for t in range(n_ax):
        target_ax = (ax + 1 + t) % n_ax
        partial = partial_sum(target_ax, t == 0)
        pair_out[t] = partial[:half_rows]
        pair_own[t] = partial[half_rows:]
        if t == 0:
            pl.semaphore_wait(barrier, len(partners))
        pair_copy(t).start()
        if t >= 1:
            plane_stage(t - 1)
        if t >= 2:
            axial_stage(t - 2)
    plane_stage(n_ax - 1)
    axial_stage(n_ax - 2)

    load.wait()
    vertex = lax.broadcasted_iota(jnp.int32, (patches, vertices), 1).astype(F32)
    live = vertex < column_of(counts[...].astype(F32))
    entries = adjacency[0]
    neighbours_each = entries.shape[1]
    index = lax.broadcasted_iota(jnp.int32, (patches, 3 * patches), 1)
    incidence = jnp.zeros((patches, 3 * patches), F32)
    for e in range(neighbours_each):
        incidence += jnp.where(index == entries[:, e : e + 1], 1.0, 0.0)
    incidence = incidence.astype(BF16)
    sub = lax.broadcasted_iota(jnp.int32, (8, vertices), 0)

    axial_stage(n_ax - 1)
    total = axial_out[n_ax - 1]
    for t in range(n_ax - 1):
        axial_copy(t).wait()
        total += axial_in[t]
    source = total * wall_scale

    def ring_copies(sweep):
        return (
            remote(ring_out.at[sweep], ring_in.at[sweep, 0], ring_sems.at[sweep, 0], (ax, after)),
            remote(ring_out.at[sweep], ring_in.at[sweep, 1], ring_sems.at[sweep, 1], (ax, before)),
        )

    field = jnp.where(live, source, 0.0)
    for sweep in range(SWEEPS):
        ring_out[sweep] = field
        for copy in ring_copies(sweep):
            copy.start()
        high, low = pieces(field)
        groups = []
        for g in range(0, patches, 8):
            stack = jnp.concatenate([high[g : g + 8], low[g : g + 8]], axis=0)
            stack = jnp.concatenate([stack, stack], axis=1).astype(BF16)
            products = jnp.dot(
                stack,
                matrices[:, g * vertices : (g + 8) * vertices],
                preferred_element_type=F32,
            )
            products = products[:8] + products[8:]
            chosen = jnp.zeros((8, vertices), F32)
            for p in range(8):
                chosen = jnp.where(sub == p, products[:, p * vertices : (p + 1) * vertices], chosen)
            groups.append(chosen)
        applied = jnp.concatenate(groups, axis=0)
        for copy in ring_copies(sweep):
            copy.wait()
        around = jnp.concatenate([ring_in[sweep, 0], field, ring_in[sweep, 1]], axis=0)
        around = jnp.concatenate(pieces(around), axis=1).astype(BF16)
        near = jnp.dot(incidence, around, preferred_element_type=F32)
        near = near[:, :vertices] + near[:, vertices:]
        image = field + smoothing * (applied + coupling * (neighbours_each * field - near))
        field = jnp.where(live, field + relaxation * (source - image), 0.0)
    out[0] = field


def smooth(tiles, owner, adjacency, counts, laplacian, vertices):
    n_ax, n_az = lax.axis_size("ax"), lax.axis_size("az")
    patches = laplacian.shape[1] // vertices
    chips = n_az // 2
    block = (patches, vertices)
    half = (chips * patches, vertices)
    vmem = pl.BlockSpec(memory_space=pltpu.VMEM)
    anywhere = pl.BlockSpec(memory_space=pl.ANY)
    dma = pltpu.SemaphoreType.DMA
    return pl.pallas_call(
        functools.partial(smooth_kernel, n_ax, n_az),
        out_shape=jax.ShapeDtypeStruct((1,) + block, F32),
        in_specs=[anywhere, vmem, vmem, vmem, anywhere],
        out_specs=vmem,
        scratch_shapes=[
            pltpu.VMEM(tiles.shape, BF16),
            pltpu.VMEM(laplacian.shape, BF16),
            pltpu.VMEM((n_ax,) + half, F32),
            pltpu.VMEM((n_ax,) + half, F32),
            pltpu.VMEM((n_ax,) + half, F32),
            pltpu.VMEM((n_ax, chips) + block, F32),
            pltpu.VMEM((n_ax, chips - 1) + block, F32),
            pltpu.VMEM((n_ax,) + block, F32),
            pltpu.VMEM((n_ax,) + block, F32),
            pltpu.VMEM((SWEEPS,) + block, F32),
            pltpu.VMEM((SWEEPS, 2) + block, F32),
            dma,
            dma,
            dma((n_ax, 2)),
            dma((n_ax, chips - 1, 2)),
            dma((n_ax, 2)),
            dma((SWEEPS, 2, 2)),
        ],
        compiler_params=pltpu.CompilerParams(
            collective_id=0, has_side_effects=True, vmem_limit_bytes=60 * 2**20
        ),
        name="smooth",
    )(tiles, owner, adjacency, counts, laplacian)


def halo_kernel(
    n_ax,
    n_az,
    adjoint,
    wall,
    laplacian,
    x_low,
    x_high,
    a_low,
    a_high,
    pieces_out,
    x_in,
    a_in,
    a_out,
    x_wall,
    a_wall,
    matrices,
    matrix_sem,
    stage_sems,
    x_sems,
    a_sems,
):
    ax, az = lax.axis_index("ax"), lax.axis_index("az")
    axial, sector, radial = adjoint.shape[1:]
    patches, vertices = laplacian.shape[1:3]
    above, below = ((ax + 1) % n_ax, az), ((ax + n_ax - 1) % n_ax, az)
    after, before = (ax, (az + 1) % n_az), (ax, (az + n_az - 1) % n_az)

    load = pltpu.make_async_copy(laplacian.at[0], matrices, matrix_sem)
    gathers = [
        pltpu.make_async_copy(adjoint.at[:, :, at], a_out.at[side], stage_sems.at[side])
        for side, at in enumerate((sector - 1, 0))
    ]
    for gather in gathers:
        gather.start()
    barrier = pltpu.get_barrier_semaphore()
    for partner in (above, below, after, before):
        pl.semaphore_signal(barrier, inc=1, device_id=partner, device_id_type=MESH)
    pl.semaphore_wait(barrier, 4)

    def remote(src, dst, sems, target):
        return pltpu.make_async_remote_copy(
            src_ref=src,
            dst_ref=dst,
            send_sem=sems.at[0],
            recv_sem=sems.at[1],
            device_id=target,
            device_id_type=MESH,
        )

    def x_copies(side):
        layer = adjoint.at[:, axial - 1] if side == 0 else adjoint.at[:, 0]
        target = above if side == 0 else below
        return (
            remote(layer, x_in.at[side], x_sems.at[side, 0], target),
            remote(wall, x_wall.at[side], x_sems.at[side, 1], target),
        )

    def a_copies(side):
        target = after if side == 0 else before
        return (
            remote(a_out.at[side], a_in.at[side], a_sems.at[side, 0], target),
            remote(wall, a_wall.at[side], a_sems.at[side, 1], target),
        )

    sends = (ax < n_ax - 1, ax > 0)
    takes = (ax > 0, ax < n_ax - 1)
    for side in range(2):

        @pl.when(sends[side])
        def _():
            for copy in x_copies(side):
                copy.start()

    for side in range(2):
        gathers[side].wait()
        for copy in a_copies(side):
            copy.start()

    load.start()
    load.wait()

    def split(p, carry):
        high, low = pieces(matrices[p].T)
        at = pl.multiple_of(p * vertices, vertices)
        pieces_out[:vertices, pl.ds(at, vertices)] = high.astype(BF16)
        pieces_out[vertices:, pl.ds(at, vertices)] = low.astype(BF16)
        return carry

    lax.fori_loop(0, patches, split, 0, unroll=4)

    lane = lax.broadcasted_iota(jnp.int32, (axial, radial), 1)
    for side, (target, at) in enumerate(((a_low, sector - 1), (a_high, 0))):
        for copy in a_copies(side):
            copy.wait()
        fluid = lane >= a_wall[side][:, at : at + 1]
        for c in range(3):
            target[c] = jnp.where(fluid, a_in[side, c], 0.0)

    lane = lax.broadcasted_iota(jnp.int32, (sector, radial), 1).astype(F32)
    for side, (target, at) in enumerate(((x_low, axial - 1), (x_high, 0))):

        @pl.when(sends[side])
        def _():
            for copy in x_copies(side):
                copy.wait_send()

        @pl.when(takes[side])
        def _():
            for copy in x_copies(side):
                copy.wait_recv()
            fluid = lane >= column_of(x_wall[side][at : at + 1, :].astype(F32))
            for c in range(3):
                target[c] = jnp.where(fluid, x_in[side, c], 0.0)

        @pl.when(jnp.logical_not(takes[side]))
        def _():
            target[...] = jnp.zeros(target.shape, F32)


def halos(adjoint, wall, laplacian):
    n_ax, n_az = lax.axis_size("ax"), lax.axis_size("az")
    comps, axial, sector, radial = adjoint.shape
    patches, vertices = laplacian.shape[1:3]
    vmem = pl.BlockSpec(memory_space=pltpu.VMEM)
    anywhere = pl.BlockSpec(memory_space=pl.ANY)
    dma = pltpu.SemaphoreType.DMA
    x_layer = (comps, sector, radial)
    a_layer = (comps, axial, radial)
    return pl.pallas_call(
        functools.partial(halo_kernel, n_ax, n_az),
        out_shape=(
            jax.ShapeDtypeStruct(x_layer, F32),
            jax.ShapeDtypeStruct(x_layer, F32),
            jax.ShapeDtypeStruct(a_layer, F32),
            jax.ShapeDtypeStruct(a_layer, F32),
            jax.ShapeDtypeStruct((2 * vertices, patches * vertices), BF16),
        ),
        in_specs=[anywhere, vmem, anywhere],
        out_specs=(vmem,) * 5,
        scratch_shapes=[
            pltpu.VMEM((2,) + x_layer, F32),
            pltpu.VMEM((2,) + a_layer, F32),
            pltpu.VMEM((2,) + a_layer, F32),
            pltpu.VMEM((2,) + wall.shape, jnp.int32),
            pltpu.VMEM((2,) + wall.shape, jnp.int32),
            pltpu.VMEM(laplacian.shape[1:], F32),
            dma,
            dma((2,)),
            dma((2, 2, 2)),
            dma((2, 2, 2)),
        ],
        compiler_params=pltpu.CompilerParams(
            collective_id=1, has_side_effects=True, vmem_limit_bytes=60 * 2**20
        ),
        name="halos",
    )(adjoint, wall, laplacian)


def shards(adjoint, primal, wall, owner, adjacency, counts, laplacian):
    vertices = laplacian.shape[2]
    *layers, matrices = halos(adjoint, wall, laplacian)
    updated, tiles = stencil(adjoint, primal, wall, layers, vertices)
    tiles = tiles.reshape(-1, 2 * vertices)
    return updated, smooth(tiles, owner, adjacency, counts, matrices, vertices)


def solution(mesh):
    in_specs = (
        P(None, "ax", "az", None),
        P(None, "ax", "az", None),
        P("ax", "az"),
        P("ax", "az"),
        P("ax", "az", None),
        P("ax", "az"),
        P("ax", "az", None, None),
    )
    out_specs = (P(None, "ax", "az", None), P("ax", "az", None))
    return jax.shard_map(shards, mesh=mesh, in_specs=in_specs, out_specs=out_specs, check_vma=False)
```

profile of v0, /device:TPU:0, one launch (start us, length us, event | category | flops | bytes accessed | tf_op | source)
XLA Modules:
  0.0 51.8 jit_solution(14685788684696897078)
XLA Ops:
  0.6 12.8 %halos.1 = (f32[3,64,256]{2,1,0:T(8,128)}, f32[3,64,256]{2,1,0:T(8,128)}, f32[3,32,256]{2,1,0:T(8,128)}, f32[3,32,256]{2,1,0:T(8,128)}, bf16[256,4096]{1,0:T(8,128)(2,1)}) custom-call(f32[3,32,64,256]{3,2,1,0:T(8,128)} %adjoint.3, s32[32,64]{1,0:T(8,128)} %wall.3, f32[1,32,128,128]{3,2,1,0:T(8,128)} %laplacian.1), custom_call_target="tpu_custom_call" | custom-call | tf_op jit(solution)/shard_map/halos/pallas_call | solution.py:532
  13.4 0.0 copy-start
  13.4 12.7 %stencil.1 = (f32[3,32,64,256]{3,2,1,0:T(8,128)}, bf16[16,2,64,256]{3,2,1,0:T(8,128)(2,1)}) custom-call(f32[3,32,64,256]{3,2,1,0:T(8,128)} %adjoint.3, f32[3,32,64,256]{3,2,1,0:T(8,128)} %primal.1, s32[32,64]{1,0:T(8,128)} %wall.3, f32[3,64,256]{2,1,0:T(8,128)} %get-tuple-element.9.x_low, f32[3,64,256]{2,1,0:T(8,128)} %get-tuple-element.10.x_high, ...), custom_call_target="tpu_custom_call" | custom-call | flops 94371840 | bytes 22020096 | tf_op jit(solution)/shard_map/stencil/pallas_call | solution.py:145
  26.1 0.0 copy-done
  26.1 0.7 %copy.9.adjacency = s32[1,32,4]{2,1,0:T(8,128)} copy(s32[1,32,4]{1,2,0:T(4,128)S(1)} %copy-done) | data formatting | bytes 1024 | tf_op args[4]
  26.8 23.6 %smooth.1 = f32[1,32,128]{2,1,0:T(8,128)} custom-call(bf16[2048,256]{1,0:T(8,128)(2,1)} %bitcast.1, s32[32,64]{1,0:T(8,128)} %owner.1, s32[1,32,4]{2,1,0:T(8,128)} %copy.9.adjacency, s32[1,32]{1,0:T(1,128)} %counts.1, bf16[256,4096]{1,0:T(8,128)(2,1)} %get-tuple-element.15.laplacian), custom_call_target="tpu_custom_call" | custom-call | tf_op jit(solution)/shard_map/smooth/pallas_call | solution.py:372
  50.5 1.3 %copy.11 = f32[1,32,128]{2,1,0:T(8,128)} copy(f32[1,32,128]{2,1,0:T(8,128)} %smooth.1) | data formatting | bytes 32768
Async XLA Ops:
  13.4 12.7 %copy-start = (s32[1,32,4]{1,2,0:T(4,128)S(1)}, s32[1,32,4]{1,2,0:T(4,128)}, u32[]{:S(2)}) copy-start(s32[1,32,4]{1,2,0:T(4,128)} %param.11) | copy-start | bytes 1540
where the time goes:
time: 52.3 us; the launch traced here: 51.8 us
  Pallas kernels  49.1 us (94%)
  local copies, waits for them, and re-layouts  2.02 us (4%)
  between operations  0.67 us (1%)
    pallas_call x1, Pallas kernels, smooth(): pl.pallas_call(functools.partial(smooth_kernel, n_ax, n_az), out_shape=ja...  23.6 us
    pallas_call x1, Pallas kernels, halos(): pl.pallas_call(functools.partial(halo_kernel, n_ax, n_az), out_shape=(jax...  12.8 us
    pallas_call x1, Pallas kernels, stencil(): pl.pallas_call(functools.partial(stencil_kernel, planes), grid=(steps,),...  12.7 us
    unnamed x4, local copies, waits for them, and re-layouts  2.02 us

commit v1 on v0

--- a/solution.py
+++ b/solution.py
@@ -34,11 +34,25 @@
 
 
 def stencil_kernel(
-    planes, adjoint, primal, wall, x_low, x_high, a_low, a_high, out, tiles, held, depth_of, sems
+    planes,
+    adjoint,
+    primal,
+    wall,
+    owner,
+    x_low,
+    x_high,
+    a_low,
+    a_high,
+    out,
+    sums,
+    held,
+    depth_of,
+    tiles,
+    sems,
 ):
     step = pl.program_id(0)
     axial, sector, radial = adjoint.shape[1:]
-    vertices = tiles.shape[-1] // 2
+    vertices = sums.shape[1]
     rows = 8
 
     def fetch(x):
@@ -131,13 +145,24 @@
             highs.append(high)
             lows.append(low)
         both = [jnp.concatenate(part, axis=0) for part in (highs, lows)]
-        tiles[j, 0] = jnp.concatenate(both, axis=1).astype(BF16)
+        at = pl.multiple_of(j * sector, sector)
+        tiles[pl.ds(at, sector), :] = jnp.concatenate(both, axis=1).astype(BF16)
         return carry
 
     lax.fori_loop(0, planes, plane, 0)
 
-
-def stencil(adjoint, primal, wall, halos, vertices):
+    owners = [owner[pl.ds(step * planes + j, 1), :] for j in range(planes)]
+    owners = jnp.concatenate(owners, axis=1)
+    chunk = 256
+    row = lax.broadcasted_iota(jnp.int32, (chunk, planes * sector), 0)
+    for at in range(0, sums.shape[0], chunk):
+        hits = jnp.where(row + at == owners, 1.0, 0.0).astype(BF16)
+        both = jnp.dot(hits, tiles[...], preferred_element_type=F32)
+        both = both[:, :vertices] + both[:, vertices:]
+        sums[at : at + chunk, :] = both + jnp.where(step > 0, sums[at : at + chunk, :], 0.0)
+
+
+def stencil(adjoint, primal, wall, owner, halos, patches_all, vertices):
     comps, axial, sector, radial = adjoint.shape
     planes = 4
     steps = axial // planes
@@ -147,7 +172,7 @@
         grid=(steps,),
         out_shape=(
             jax.ShapeDtypeStruct(adjoint.shape, F32),
-            jax.ShapeDtypeStruct((axial // 2, 2, sector, 2 * vertices), BF16),
+            jax.ShapeDtypeStruct((patches_all, vertices), F32),
         ),
         in_specs=[
             pl.BlockSpec(memory_space=pl.ANY),
@@ -157,40 +182,35 @@
             vmem,
             vmem,
             vmem,
+            vmem,
         ],
         out_specs=(
             pl.BlockSpec((comps, planes, sector, radial), lambda i: (0, i, 0, 0)),
-            pl.BlockSpec(
-                (planes, 1, sector, 2 * vertices),
-                lambda i: (i % (steps // 2), i // (steps // 2), 0, 0),
-            ),
+            pl.BlockSpec((patches_all, vertices), lambda i: (0, 0)),
         ),
         scratch_shapes=[
             pltpu.VMEM((comps, axial + 2, sector + 2 * PAD, radial), F32),
             pltpu.VMEM((axial + 1, sector, vertices), F32),
+            pltpu.VMEM((planes * sector, 2 * vertices), BF16),
             pltpu.SemaphoreType.DMA((axial,)),
         ],
-        compiler_params=pltpu.CompilerParams(vmem_limit_bytes=60 * 2**20),
+        compiler_params=pltpu.CompilerParams(vmem_limit_bytes=46 * 2**20),
         cost_estimate=pl.CostEstimate(
             flops=60 * adjoint.size, bytes_accessed=14 * adjoint.size, transcendentals=0
         ),
         name="stencil",
-    )(adjoint, primal, wall, *halos)
+    )(adjoint, primal, wall, owner, *halos)
 
 
 def smooth_kernel(
     n_ax,
     n_az,
-    tiles_in,
-    owner,
+    sums,
     adjacency,
     counts,
     laplacian,
     out,
-    tiles,
     matrices,
-    pair_out,
-    pair_own,
     pair_in,
     plane_sum,
     plane_in,
@@ -198,7 +218,6 @@
     axial_in,
     ring_out,
     ring_in,
-    tile_sem,
     matrix_sem,
     pair_sems,
     plane_sems,
@@ -211,10 +230,7 @@
     chip, core = az // 2, az % 2
     sibling = chip * 2 + (1 - core)
     after, before = (az + 1) % n_az, (az + n_az - 1) % n_az
-    half_rows = chips * patches
-
-    tile_load = pltpu.make_async_copy(tiles_in, tiles, tile_sem)
-    tile_load.start()
+
     load = pltpu.make_async_copy(laplacian, matrices, matrix_sem)
     load.start()
 
@@ -224,25 +240,6 @@
     partners += [((ax + d) % n_ax, az) for d in range(1, n_ax)]
     for partner in partners:
         pl.semaphore_signal(barrier, inc=1, device_id=partner, device_id_type=MESH)
-
-    columns_half = owner.shape[0] // 2
-    owners = jnp.concatenate([owner[:columns_half, :], owner[columns_half:, :]], axis=1)
-    width = owners.shape[1]
-    row = lax.broadcasted_iota(jnp.int32, (2 * half_rows, width), 0)
-    row_core = jnp.where(row < half_rows, 1 - core, core)
-    row_chip = (row % half_rows) // patches
-    row_patch = (row_chip * 2 + row_core) * patches + row % patches
-
-    def partial_sum(target_ax, first):
-        ids = row_patch + target_ax * n_az * patches
-        hits = [
-            jnp.where(ids == owners[b : b + 1, :], 1.0, 0.0).astype(BF16)
-            for b in range(columns_half)
-        ]
-        if first:
-            tile_load.wait()
-        both = jnp.dot(jnp.concatenate(hits, axis=1), tiles[...], preferred_element_type=F32)
-        return both[:, :vertices] + both[:, vertices:]
 
     def remote(src, dst, sems, target):
         return pltpu.make_async_remote_copy(
@@ -255,7 +252,8 @@
         )
 
     def pair_copy(t):
-        return remote(pair_out.at[t], pair_in.at[t], pair_sems.at[t], (ax, sibling))
+        layer = sums.at[(ax + 1 + t) % n_ax, :, 1 - core]
+        return remote(layer, pair_in.at[t], pair_sems.at[t], (ax, sibling))
 
     def plane_copy(t, d):
         target = (chip + d) % chips
@@ -273,8 +271,7 @@
 
     def plane_stage(t):
         pair_copy(t).wait()
-        joined = pair_own[t] + pair_in[t]
-        plane_sum[t] = joined.reshape(chips, patches, vertices)
+        plane_sum[t] = sums[(ax + 1 + t) % n_ax, :, core] + pair_in[t]
         for d in range(1, chips):
             plane_copy(t, d).start()
 
@@ -288,20 +285,13 @@
         if t < n_ax - 1:
             axial_copy(t).start()
 
+    pl.semaphore_wait(barrier, len(partners))
     for t in range(n_ax):
-        target_ax = (ax + 1 + t) % n_ax
-        partial = partial_sum(target_ax, t == 0)
-        pair_out[t] = partial[:half_rows]
-        pair_own[t] = partial[half_rows:]
-        if t == 0:
-            pl.semaphore_wait(barrier, len(partners))
         pair_copy(t).start()
+    for t in range(n_ax):
+        plane_stage(t)
         if t >= 1:
-            plane_stage(t - 1)
-        if t >= 2:
-            axial_stage(t - 2)
-    plane_stage(n_ax - 1)
-    axial_stage(n_ax - 2)
+            axial_stage(t - 1)
 
     load.wait()
     vertex = lax.broadcasted_iota(jnp.int32, (patches, vertices), 1).astype(F32)
@@ -360,26 +350,23 @@
     out[0] = field
 
 
-def smooth(tiles, owner, adjacency, counts, laplacian, vertices):
+def smooth(sums, adjacency, counts, laplacian):
     n_ax, n_az = lax.axis_size("ax"), lax.axis_size("az")
-    patches = laplacian.shape[1] // vertices
     chips = n_az // 2
+    patches, vertices = counts.shape[1], sums.shape[1]
+    sums = sums.reshape(n_ax, chips, 2, patches, vertices)
     block = (patches, vertices)
-    half = (chips * patches, vertices)
     vmem = pl.BlockSpec(memory_space=pltpu.VMEM)
     anywhere = pl.BlockSpec(memory_space=pl.ANY)
     dma = pltpu.SemaphoreType.DMA
     return pl.pallas_call(
         functools.partial(smooth_kernel, n_ax, n_az),
         out_shape=jax.ShapeDtypeStruct((1,) + block, F32),
-        in_specs=[anywhere, vmem, vmem, vmem, anywhere],
+        in_specs=[vmem, vmem, vmem, anywhere],
         out_specs=vmem,
         scratch_shapes=[
-            pltpu.VMEM(tiles.shape, BF16),
             pltpu.VMEM(laplacian.shape, BF16),
-            pltpu.VMEM((n_ax,) + half, F32),
-            pltpu.VMEM((n_ax,) + half, F32),
-            pltpu.VMEM((n_ax,) + half, F32),
+            pltpu.VMEM((n_ax, chips) + block, F32),
             pltpu.VMEM((n_ax, chips) + block, F32),
             pltpu.VMEM((n_ax, chips - 1) + block, F32),
             pltpu.VMEM((n_ax,) + block, F32),
@@ -387,17 +374,16 @@
             pltpu.VMEM((SWEEPS,) + block, F32),
             pltpu.VMEM((SWEEPS, 2) + block, F32),
             dma,
-            dma,
             dma((n_ax, 2)),
             dma((n_ax, chips - 1, 2)),
             dma((n_ax, 2)),
             dma((SWEEPS, 2, 2)),
         ],
         compiler_params=pltpu.CompilerParams(
-            collective_id=0, has_side_effects=True, vmem_limit_bytes=60 * 2**20
+            collective_id=0, has_side_effects=True, vmem_limit_bytes=40 * 2**20
         ),
         name="smooth",
-    )(tiles, owner, adjacency, counts, laplacian)
+    )(sums, adjacency, counts, laplacian)
 
 
 def halo_kernel(
@@ -553,7 +539,10 @@
             dma((2, 2, 2)),
         ],
         compiler_params=pltpu.CompilerParams(
-            collective_id=1, has_side_effects=True, vmem_limit_bytes=60 * 2**20
+            collective_id=1, has_side_effects=True, vmem_limit_bytes=57 * 2**20
+        ),
+        cost_estimate=pl.CostEstimate(
+            flops=0, bytes_accessed=8 * adjoint.size * 4, transcendentals=0
         ),
         name="halos",
     )(adjoint, wall, laplacian)
@@ -562,9 +551,9 @@
 def shards(adjoint, primal, wall, owner, adjacency, counts, laplacian):
     vertices = laplacian.shape[2]
     *layers, matrices = halos(adjoint, wall, laplacian)
-    updated, tiles = stencil(adjoint, primal, wall, layers, vertices)
-    tiles = tiles.reshape(-1, 2 * vertices)
-    return updated, smooth(tiles, owner, adjacency, counts, matrices, vertices)
+    patches_all = lax.axis_size("ax") * lax.axis_size("az") * laplacian.shape[1]
+    updated, sums = stencil(adjoint, primal, wall, owner, layers, patches_all, vertices)
+    return updated, smooth(sums, adjacency, counts, matrices)
 
 
 def solution(mesh):

time: 52.3 us -> 58.2 us (1.11)
  local copies, waits for them, and re-layouts: 2.02 us -> 5.94 us
  Pallas kernels: 49.1 us -> 51.1 us
    unnamed x4 -> x22, local copies, waits for them, and re-layouts: 2.02 us -> 5.94 us
    pallas_call x1, Pallas kernels: 12.7 us -> 16 us  [stencil(): pl.pallas_call(functools.partial(stencil_kernel, planes), grid=(steps,),...]
    pallas_call x1, Pallas kernels: 23.6 us -> 22.1 us  [smooth(): pl.pallas_call(functools.partial(smooth_kernel, n_ax, n_az), out_shape=ja...]
where the time goes in v1:
time: 58.2 us; the launch traced here: 57.7 us
  Pallas kernels  51.1 us (88%)
  local copies, waits for them, and re-layouts  5.94 us (10%)
  between operations  0.72 us (1%)
    pallas_call x1, Pallas kernels, smooth(): pl.pallas_call(functools.partial(smooth_kernel, n_ax, n_az), out_shape=ja...  22.1 us
    pallas_call x1, Pallas kernels, stencil(): pl.pallas_call(functools.partial(stencil_kernel, planes), grid=(steps,),...  16 us
    pallas_call x1, Pallas kernels, halos(): pl.pallas_call(functools.partial(halo_kernel, n_ax, n_az), out_shape=(jax...  12.9 us
    unnamed x22, local copies, waits for them, and re-layouts  5.94 us

profile of v1, /device:TPU:0, one launch (start us, length us, event | category | flops | bytes accessed | tf_op | source)
XLA Modules:
  0.0 57.7 jit_solution(6087026394158814524)
XLA Ops:
  0.6 0.0 copy-start
  0.6 0.0 copy-start.6
  0.7 0.0 copy-start.7
  0.7 12.9 %halos.1 = (f32[3,64,256]{2,1,0:T(8,128)}, f32[3,64,256]{2,1,0:T(8,128)}, f32[3,32,256]{2,1,0:T(8,128)}, f32[3,32,256]{2,1,0:T(8,128)}, bf16[256,4096]{1,0:T(8,128)(2,1)}) custom-call(f32[3,32,64,256]{3,2,1,0:T(8,128)} %adjoint.3, s32[32,64]{1,0:T(8,128)} %wall.3, f32[1,32,128,128]{3,2,1,0:T(8,128)} %laplacian.1), custom_call_target="tpu_custom_call" | custom-call | bytes 50331648 | tf_op jit(solution)/shard_map/halos/pallas_call | solution.py:518
  13.6 0.0 copy-done
  13.6 0.0 copy-done.6
  13.6 0.0 copy-done.7
  13.6 0.0 copy-start.2
  13.6 0.9 %copy-done.2 = f32[3,64,256]{2,1,0:T(8,128)S(1)} copy-done((f32[3,64,256]{2,1,0:T(8,128)S(1)}, f32[3,64,256]{2,1,0:T(8,128)}, u32[]{:S(2)}) %copy-start.2) | copy-done | bytes 196632
  14.5 0.0 copy-start.3
  14.5 0.9 %copy-done.3 = f32[3,64,256]{2,1,0:T(8,128)S(1)} copy-done((f32[3,64,256]{2,1,0:T(8,128)S(1)}, f32[3,64,256]{2,1,0:T(8,128)}, u32[]{:S(2)}) %copy-start.3) | copy-done | bytes 196632
  15.5 0.0 copy-start.4
  15.5 0.9 %copy-done.4 = f32[3,32,256]{2,1,0:T(8,128)S(1)} copy-done((f32[3,32,256]{2,1,0:T(8,128)S(1)}, f32[3,32,256]{2,1,0:T(8,128)}, u32[]{:S(2)}) %copy-start.4) | copy-done | bytes 98328
  16.4 0.0 copy-start.5
  16.4 0.9 %copy-done.5 = f32[3,32,256]{2,1,0:T(8,128)S(1)} copy-done((f32[3,32,256]{2,1,0:T(8,128)S(1)}, f32[3,32,256]{2,1,0:T(8,128)}, u32[]{:S(2)}) %copy-start.5) | copy-done | bytes 98328
  17.3 0.0 copy-start.9
  17.3 0.0 copy-start.8
  17.3 16.0 %stencil.1 = (f32[3,32,64,256]{3,2,1,0:T(8,128)}, f32[1024,128]{1,0:T(8,128)S(1)}) custom-call(f32[3,32,64,256]{3,2,1,0:T(8,128)S(1)} %copy-done, f32[3,32,64,256]{3,2,1,0:T(8,128)} %primal.1, s32[32,64]{1,0:T(8,128)S(1)} %copy-done.6, s32[32,64]{1,0:T(8,128)S(1)} %copy-done.7, f32[3,64,256]{2,1,0:T(8,128)S(1)} %copy-done.2, f32[3,64,256]{2,1,0:T(8,128)S(1)} %copy-done.3, ...), custom_call_target="tpu_custom_call" | custom-call | flops 94371840 | bytes 22020096 | tf_op jit(solution)/shard_map/stencil/pallas_call | solution.py:170
  33.3 0.0 copy-done.9
  33.3 0.1 copy.9.adjacency
  33.4 0.0 copy-done.8
  33.4 1.6 %copy-done.1 = bf16[256,4096]{1,0:T(8,128)(2,1)S(1)} copy-done((bf16[256,4096]{1,0:T(8,128)(2,1)S(1)}, bf16[256,4096]{1,0:T(8,128)(2,1)}, u32[]{:S(2)}) %copy-start.1) | copy-done | bytes 2097176
  35.0 22.1 %smooth.1 = f32[1,32,128]{2,1,0:T(8,128)S(1)} custom-call(f32[4,4,2,32,128]{4,3,2,1,0:T(8,128)S(1)} %bitcast.1, s32[1,32,4]{2,1,0:T(8,128)S(1)} %copy.9.adjacency, s32[1,32]{1,0:T(1,128)S(1)} %copy-done.8, bf16[256,4096]{1,0:T(8,128)(2,1)S(1)} %copy-done.1), custom_call_target="tpu_custom_call" | custom-call | tf_op jit(solution)/shard_map/smooth/pallas_call | solution.py:362
  57.1 0.6 %copy.11 = f32[1,32,128]{2,1,0:T(8,128)} copy(f32[1,32,128]{2,1,0:T(8,128)S(1)} %smooth.1) | data formatting | bytes 32768
  (1 shorter events, 0.0 us)
Async XLA Ops:
  0.6 13.0 %copy-start = (f32[3,32,64,256]{3,2,1,0:T(8,128)S(1)}, f32[3,32,64,256]{3,2,1,0:T(8,128)}, u32[]{:S(2)}) copy-start(f32[3,32,64,256]{3,2,1,0:T(8,128)} %adjoint.3) | copy-start | bytes 18874372
  0.6 13.0 %copy-start.6 = (s32[32,64]{1,0:T(8,128)S(1)}, s32[32,64]{1,0:T(8,128)}, u32[]{:S(2)}) copy-start(s32[32,64]{1,0:T(8,128)} %wall.3) | copy-start | bytes 24580
  0.7 13.0 %copy-start.7 = (s32[32,64]{1,0:T(8,128)S(1)}, s32[32,64]{1,0:T(8,128)}, u32[]{:S(2)}) copy-start(s32[32,64]{1,0:T(8,128)} %owner.1) | copy-start | bytes 24580
  13.6 0.9 %copy-start.2 = (f32[3,64,256]{2,1,0:T(8,128)S(1)}, f32[3,64,256]{2,1,0:T(8,128)}, u32[]{:S(2)}) copy-start(f32[3,64,256]{2,1,0:T(8,128)} %get-tuple-element.9.x_low) | copy-start | bytes 589828
  14.5 0.9 %copy-start.3 = (f32[3,64,256]{2,1,0:T(8,128)S(1)}, f32[3,64,256]{2,1,0:T(8,128)}, u32[]{:S(2)}) copy-start(f32[3,64,256]{2,1,0:T(8,128)} %get-tuple-element.10.x_high) | copy-start | bytes 589828
  15.5 0.9 %copy-start.4 = (f32[3,32,256]{2,1,0:T(8,128)S(1)}, f32[3,32,256]{2,1,0:T(8,128)}, u32[]{:S(2)}) copy-start(f32[3,32,256]{2,1,0:T(8,128)} %get-tuple-element.11.a_low) | copy-start | bytes 294916
  16.4 0.9 %copy-start.5 = (f32[3,32,256]{2,1,0:T(8,128)S(1)}, f32[3,32,256]{2,1,0:T(8,128)}, u32[]{:S(2)}) copy-start(f32[3,32,256]{2,1,0:T(8,128)} %get-tuple-element.12.a_high) | copy-start | bytes 294916
  17.3 16.0 %copy-start.9 = (s32[1,32,4]{1,2,0:T(4,128)S(1)}, s32[1,32,4]{1,2,0:T(4,128)}, u32[]{:S(2)}) copy-start(s32[1,32,4]{1,2,0:T(4,128)} %param.11) | copy-start | bytes 1540
  17.3 16.1 %copy-start.8 = (s32[1,32]{1,0:T(1,128)S(1)}, s32[1,32]{1,0:T(1,128)}, u32[]{:S(2)}) copy-start(s32[1,32]{1,0:T(1,128)} %counts.1) | copy-start | bytes 388
  33.4 1.6 %copy-start.1 = (bf16[256,4096]{1,0:T(8,128)(2,1)S(1)}, bf16[256,4096]{1,0:T(8,128)(2,1)}, u32[]{:S(2)}) copy-start(bf16[256,4096]{1,0:T(8,128)(2,1)} %get-tuple-element.15.laplacian) | copy-start | bytes 6291460

commit v2 on v0

--- a/solution.py
+++ b/solution.py
@@ -51,13 +51,13 @@
             held[c, x + 1, PAD - 1 : PAD, :] = a_low[c, pl.ds(x, 1), :]
             held[c, x + 1, PAD + sector : PAD + sector + 1, :] = a_high[c, pl.ds(x, 1), :]
 
+    def begin(x, carry):
+        fetch(x).start()
+        return carry
+
     @pl.when(step == 0)
     def _():
-        def begin(x, carry):
-            fetch(x).start()
-            return carry
-
-        lax.fori_loop(0, axial, begin, 0)
+        lax.fori_loop(0, min(axial, 2 * planes + 1), begin, 0)
         for c in range(3):
             held[c, 0, PAD : PAD + sector, :] = x_low[c]
             held[c, axial + 1, PAD : PAD + sector, :] = x_high[c]
@@ -73,6 +73,13 @@
         for c in range(3):
             body = held[c, 1, PAD : PAD + sector, :]
             held[c, 1, PAD : PAD + sector, :] = jnp.where(solid, 0.0, body)
+
+    for j in range(1, planes + 1):
+        later = (step + 2) * planes + j
+
+        @pl.when(later < axial)
+        def _():
+            fetch(later).start()
 
     lane = lax.broadcasted_iota(jnp.int32, (rows, radial), 1)
     sub = lax.broadcasted_iota(jnp.int32, (rows, radial), 0)
@@ -181,13 +188,12 @@
 def smooth_kernel(
     n_ax,
     n_az,
-    tiles_in,
+    tiles,
     owner,
     adjacency,
     counts,
     laplacian,
     out,
-    tiles,
     matrices,
     pair_out,
     pair_own,
@@ -198,7 +204,6 @@
     axial_in,
     ring_out,
     ring_in,
-    tile_sem,
     matrix_sem,
     pair_sems,
     plane_sems,
@@ -213,8 +218,6 @@
     after, before = (az + 1) % n_az, (az + n_az - 1) % n_az
     half_rows = chips * patches
 
-    tile_load = pltpu.make_async_copy(tiles_in, tiles, tile_sem)
-    tile_load.start()
     load = pltpu.make_async_copy(laplacian, matrices, matrix_sem)
     load.start()
 
@@ -233,14 +236,12 @@
     row_chip = (row % half_rows) // patches
     row_patch = (row_chip * 2 + row_core) * patches + row % patches
 
-    def partial_sum(target_ax, first):
+    def partial_sum(target_ax):
         ids = row_patch + target_ax * n_az * patches
         hits = [
             jnp.where(ids == owners[b : b + 1, :], 1.0, 0.0).astype(BF16)
             for b in range(columns_half)
         ]
-        if first:
-            tile_load.wait()
         both = jnp.dot(jnp.concatenate(hits, axis=1), tiles[...], preferred_element_type=F32)
         return both[:, :vertices] + both[:, vertices:]
 
@@ -290,7 +291,7 @@
 
     for t in range(n_ax):
         target_ax = (ax + 1 + t) % n_ax
-        partial = partial_sum(target_ax, t == 0)
+        partial = partial_sum(target_ax)
         pair_out[t] = partial[:half_rows]
         pair_own[t] = partial[half_rows:]
         if t == 0:
@@ -367,15 +368,13 @@
     block = (patches, vertices)
     half = (chips * patches, vertices)
     vmem = pl.BlockSpec(memory_space=pltpu.VMEM)
-    anywhere = pl.BlockSpec(memory_space=pl.ANY)
     dma = pltpu.SemaphoreType.DMA
     return pl.pallas_call(
         functools.partial(smooth_kernel, n_ax, n_az),
         out_shape=jax.ShapeDtypeStruct((1,) + block, F32),
-        in_specs=[anywhere, vmem, vmem, vmem, anywhere],
+        in_specs=[vmem, vmem, vmem, vmem, pl.BlockSpec(memory_space=pl.ANY)],
         out_specs=vmem,
         scratch_shapes=[
-            pltpu.VMEM(tiles.shape, BF16),
             pltpu.VMEM(laplacian.shape, BF16),
             pltpu.VMEM((n_ax,) + half, F32),
             pltpu.VMEM((n_ax,) + half, F32),
@@ -387,14 +386,13 @@
             pltpu.VMEM((SWEEPS,) + block, F32),
             pltpu.VMEM((SWEEPS, 2) + block, F32),
             dma,
-            dma,
             dma((n_ax, 2)),
             dma((n_ax, chips - 1, 2)),
             dma((n_ax, 2)),
             dma((SWEEPS, 2, 2)),
         ],
         compiler_params=pltpu.CompilerParams(
-            collective_id=0, has_side_effects=True, vmem_limit_bytes=60 * 2**20
+            collective_id=0, has_side_effects=True, vmem_limit_bytes=40 * 2**20
         ),
         name="smooth",
     )(tiles, owner, adjacency, counts, laplacian)

time: 52.3 us -> 51.5 us (0.985)
  Pallas kernels: 49.1 us -> 48.4 us
    pallas_call x1, Pallas kernels: 23.6 us -> 22.8 us  [smooth(): pl.pallas_call(functools.partial(smooth_kernel, n_ax, n_az), out_shape=ja...]
    unnamed x4 -> x12, local copies, waits for them, and re-layouts: 2.02 us -> 1.94 us
where the time goes in v2:
time: 51.5 us; the launch traced here: 51 us
  Pallas kernels  48.4 us (94%)
  local copies, waits for them, and re-layouts  1.94 us (4%)
  between operations  0.71 us (1%)
    pallas_call x1, Pallas kernels, smooth(): pl.pallas_call(functools.partial(smooth_kernel, n_ax, n_az), out_shape=ja...  22.8 us
    pallas_call x1, Pallas kernels, stencil(): pl.pallas_call(functools.partial(stencil_kernel, planes), grid=(steps,),...  12.8 us
    pallas_call x1, Pallas kernels, halos(): pl.pallas_call(functools.partial(halo_kernel, n_ax, n_az), out_shape=(jax...  12.8 us
    unnamed x12, local copies, waits for them, and re-layouts  1.94 us

profile of v2, /device:TPU:0, one launch (start us, length us, event | category | flops | bytes accessed | tf_op | source)
XLA Modules:
  0.0 51.0 jit_solution(15259569688985804412)
XLA Ops:
  0.6 12.8 %halos.1 = (f32[3,64,256]{2,1,0:T(8,128)}, f32[3,64,256]{2,1,0:T(8,128)}, f32[3,32,256]{2,1,0:T(8,128)}, f32[3,32,256]{2,1,0:T(8,128)}, bf16[256,4096]{1,0:T(8,128)(2,1)}) custom-call(f32[3,32,64,256]{3,2,1,0:T(8,128)} %adjoint.3, s32[32,64]{1,0:T(8,128)} %wall.3, f32[1,32,128,128]{3,2,1,0:T(8,128)} %laplacian.1), custom_call_target="tpu_custom_call" | custom-call | tf_op jit(solution)/shard_map/halos/pallas_call | solution.py:530
  13.4 0.0 copy-start.4
  13.4 0.0 copy-start
  13.4 0.0 copy-start.2
  13.4 0.0 copy-start.3
  13.5 12.8 %stencil.1 = (f32[3,32,64,256]{3,2,1,0:T(8,128)}, bf16[16,2,64,256]{3,2,1,0:T(8,128)(2,1)}) custom-call(f32[3,32,64,256]{3,2,1,0:T(8,128)} %adjoint.3, f32[3,32,64,256]{3,2,1,0:T(8,128)} %primal.1, s32[32,64]{1,0:T(8,128)} %wall.3, f32[3,64,256]{2,1,0:T(8,128)} %get-tuple-element.9.x_low, f32[3,64,256]{2,1,0:T(8,128)} %get-tuple-element.10.x_high, ...), custom_call_target="tpu_custom_call" | custom-call | flops 94371840 | bytes 22020096 | tf_op jit(solution)/shard_map/stencil/pallas_call | solution.py:152
  26.3 0.0 copy-done.4
  26.3 0.1 copy.9.adjacency
  26.4 0.0 copy-done
  26.4 0.0 copy-done.2
  26.4 0.0 copy-done.3
  26.4 0.0 copy-start.1
  26.4 1.2 %copy-done.1 = bf16[16,2,64,256]{3,2,1,0:T(8,128)(2,1)S(1)} copy-done((bf16[16,2,64,256]{3,2,1,0:T(8,128)(2,1)S(1)}, bf16[16,2,64,256]{3,2,1,0:T(8,128)(2,1)}, u32[]{:S(2)}) %copy-start.1) | copy-done | bytes 1048600
  27.6 22.8 %smooth.1 = f32[1,32,128]{2,1,0:T(8,128)S(1)} custom-call(bf16[2048,256]{1,0:T(8,128)(2,1)S(1)} %bitcast.1, s32[32,64]{1,0:T(8,128)S(1)} %copy-done.2, s32[1,32,4]{2,1,0:T(8,128)S(1)} %copy.9.adjacency, s32[1,32]{1,0:T(1,128)S(1)} %copy-done.3, bf16[256,4096]{1,0:T(8,128)(2,1)S(1)} %copy-done), custom_call_target="tpu_custom_call" | custom-call | tf_op jit(solution)/shard_map/smooth/pallas_call | solution.py:372
  50.4 0.6 %copy.11 = f32[1,32,128]{2,1,0:T(8,128)} copy(f32[1,32,128]{2,1,0:T(8,128)S(1)} %smooth.1) | data formatting | bytes 32768
Async XLA Ops:
  13.4 12.9 %copy-start.4 = (s32[1,32,4]{1,2,0:T(4,128)S(1)}, s32[1,32,4]{1,2,0:T(4,128)}, u32[]{:S(2)}) copy-start(s32[1,32,4]{1,2,0:T(4,128)} %param.11) | copy-start | bytes 1540
  13.4 13.0 %copy-start = (bf16[256,4096]{1,0:T(8,128)(2,1)S(1)}, bf16[256,4096]{1,0:T(8,128)(2,1)}, u32[]{:S(2)}) copy-start(bf16[256,4096]{1,0:T(8,128)(2,1)} %get-tuple-element.15.laplacian) | copy-start | bytes 6291460
  13.4 13.0 %copy-start.2 = (s32[32,64]{1,0:T(8,128)S(1)}, s32[32,64]{1,0:T(8,128)}, u32[]{:S(2)}) copy-start(s32[32,64]{1,0:T(8,128)} %owner.1) | copy-start | bytes 24580
  13.4 13.0 %copy-start.3 = (s32[1,32]{1,0:T(1,128)S(1)}, s32[1,32]{1,0:T(1,128)}, u32[]{:S(2)}) copy-start(s32[1,32]{1,0:T(1,128)} %counts.1) | copy-start | bytes 388
  26.4 1.2 %copy-start.1 = (bf16[16,2,64,256]{3,2,1,0:T(8,128)(2,1)S(1)}, bf16[16,2,64,256]{3,2,1,0:T(8,128)(2,1)}, u32[]{:S(2)}) copy-start(bf16[16,2,64,256]{3,2,1,0:T(8,128)(2,1)} %get-tuple-element.14) | copy-start | bytes 3145732
